TPU v7x, 768 devices: a whole 4x8x12 slice. The times are simulated.
768 devices in a mesh: grp: 24 (over z, core), shard: 32 (over x, y).
Axes of the slice: x: 4, y: 8, z: 12, core: 2. Of those that a mesh axis runs over, the one named last changes fastest.
Arguments:
- points: bfloat16 [196608, 4096], P(('grp', 'shard'))
- centroids: bfloat16 [128, 168, 4096], P('shard', 'grp')
- candidates: int32 [768, 2], P('grp'), may hold values from 0 to 167
- assign: int32 [196608], P(('grp', 'shard')), may hold values from 0 to 3071, as said below
- slot_index: int32 [196608], P(('grp', 'shard')), may hold values from 0 to 127, as said below
Outputs:
- cand_scores: float32 [196608, 256], P(('grp', 'shard'))
- gram: float32 [3072, 128, 128], P(('grp', 'shard'))
- member_best: float32 [196608], P(('grp', 'shard'))
Inputs may be any that keep to these rules, and one draw needn't show every extreme that they name: `candidates`: tile numbers of the candidate lists; a list may name a tile twice. `assign`: the points of group index g of grp are assigned to clusters g * 32 * 4 to (g + 1) * 32 * 4 - 1; cluster c is owned by device c // 4 in grp+shard order. The points of one device fall on the clusters of one owner at most 12 times, and on one cluster at most 12 // 4 times; both bounds are reached in every draw. `slot_index`: within one cluster the members' slot indices are distinct; every cluster uses slot 127.
All inputs are finite; a program needn't handle non-finite values.
Results may differ from a plain program's by a relative error of at most 0.0003.
Values may be sent and summed in bfloat16 or wider, within the bound.
A program may use at most 64 MiB of HBM per device.

v0:
```python
import math

import jax
import jax.numpy as jnp
from jax import lax
from jax.sharding import PartitionSpec as P

D = 4096
TILE = 128
K = 2
CAP = 128


eps = 1e-06
score_scale = 64.0


def inverse_norm(row_data):
    mean_square = jnp.mean(jnp.square(row_data.astype(jnp.float32)), axis=-1)
    return lax.rsqrt(mean_square + eps) / math.sqrt(row_data.shape[-1])


def on_device(points, centroids, candidates, assign, slot_index):
    shard_count = lax.axis_size("shard")
    pts_local = points.shape[0]
    tiles_dev = pts_local // TILE
    rows_local = centroids.shape[0]
    wanted = candidates.reshape(-1)
    start_rows = jnp.zeros((rows_local, wanted.shape[0], D), jnp.bfloat16)
    piece = lax.all_gather(centroids, "grp", axis=1, tiled=True)
    count = piece.shape[1]
    inside = (wanted >= 0) & (wanted < count)
    taken = jnp.take(piece, jnp.clip(wanted, 0, count - 1), axis=1)
    outgoing = jnp.where(inside[None, :, None], taken, start_rows)
    outgoing = outgoing.reshape(rows_local, shard_count, K, D)
    point_scale = inverse_norm(points)
    arrived = lax.all_to_all(outgoing, "shard", split_axis=1, concat_axis=1, tiled=True)
    dots = jnp.einsum("nd,rpkd->nkpr", points, arrived, preferred_element_type=jnp.float32)
    column_scale = jnp.transpose(inverse_norm(arrived), (2, 1, 0))
    scaled = score_scale * dots * point_scale[:, None, None, None] * column_scale[None]
    cand_scores = scaled.reshape(pts_local, K * TILE)
    cl_dev = 2 * tiles_dev
    slot_count = 3 * cl_dev * CAP // (4 * shard_count)
    owner_id = assign // cl_dev % shard_count
    owner_hits = (owner_id[:, None] == jnp.arange(shard_count, dtype=jnp.int32)[None, :]).astype(
        jnp.int32
    )
    rank_in = jnp.sum(owner_hits * (jnp.cumsum(owner_hits, axis=0) - 1), axis=1)
    dest_row = owner_id * slot_count + rank_in
    member_id = assign % cl_dev * CAP + slot_index
    send_rows = jnp.zeros((shard_count * slot_count, D), jnp.bfloat16).at[dest_row].set(points)
    send_ids = jnp.full((shard_count * slot_count,), -1, jnp.int32).at[dest_row].set(member_id)
    got_rows, got_ids = (
        lax.all_to_all(
            send_rows.reshape(shard_count, slot_count, D),
            "shard",
            split_axis=0,
            concat_axis=0,
            tiled=True,
        ),
        lax.all_to_all(
            send_ids.reshape(shard_count, slot_count),
            "shard",
            split_axis=0,
            concat_axis=0,
            tiled=True,
        ),
    )
    flat_ids = got_ids.reshape(-1)
    placed_at = jnp.where(flat_ids >= 0, flat_ids, cl_dev * CAP)
    cluster_rows = (
        jnp.zeros((cl_dev * CAP, D), jnp.bfloat16)
        .at[placed_at]
        .set(got_rows.reshape(-1, D), mode="drop")
    )
    occupied = jnp.zeros((cl_dev * CAP,), jnp.int32).at[placed_at].set(1, mode="drop")
    cluster_rows = cluster_rows.reshape(cl_dev, CAP, D)
    inner_prod = jnp.einsum(
        "cid,cjd->cij", cluster_rows, cluster_rows, preferred_element_type=jnp.float32
    )
    unit_scale = inverse_norm(cluster_rows)
    gram_block = score_scale * inner_prod * unit_scale[:, :, None] * unit_scale[:, None, :]
    not_self = 1 - jnp.eye(CAP, dtype=jnp.int32) > 0
    others = (occupied.reshape(cl_dev, CAP)[:, None, :] > 0) & not_self[None]
    highest = jnp.max(jnp.where(others, gram_block, -jnp.inf), axis=2)
    best_row = jnp.where(jnp.any(others, axis=2), highest, 0.0).reshape(-1)
    replies = jnp.take(best_row, jnp.clip(flat_ids, 0, cl_dev * CAP - 1)).reshape(
        shard_count, slot_count
    )
    returned = lax.all_to_all(replies, "shard", split_axis=0, concat_axis=0, tiled=True)
    member_best = jnp.take(returned.reshape(-1), dest_row)
    return (cand_scores, gram_block, member_best)


def solution(mesh):
    in_specs = (
        P(("grp", "shard"), None),
        P("shard", "grp", None),
        P("grp", None),
        P(("grp", "shard")),
        P(("grp", "shard")),
    )
    out_specs = (P(("grp", "shard"), None), P(("grp", "shard"), None, None), P(("grp", "shard")))
    return jax.shard_map(
        on_device, mesh=mesh, in_specs=in_specs, out_specs=out_specs, check_vma=False
    )
```

profile of v0, /device:TPU:656, one launch (start us, length us, event | category | flops | bytes accessed | tf_op | source)
XLA Modules:
  0.0 244.3 jit_solution(10069404875925188758)
XLA Ops:
  7.2 0.7 all-gather.2.cloned.1.call-update
  7.9 0.7 fusion.30
  8.6 0.6 reduce-window.6
  9.6 1.4 scatter_custom_fusion
  11.0 0.7 all_to_all.17
  11.7 10.1 %all-to-all-start.1 = ((s32[32,1,12]{2,1,0:T(1,128)}), s32[32,1,12]{2,1,0:T(1,128)S(1)}, u32[]{:S(2)}, u32[]{:S(2)}) async-start(s32[32,1,12]{2,1,0:T(1,128)} %bitcast.9), calls=%async_computation.1 | async-start | bytes 32768 | tf_op jit(solution)/shard_map/all_to_all | solution.py:61
  21.7 5.5 %scatter_custom_fusion.1 = bf16[384,4096]{1,0:T(8,128)(2,1)S(1)} fusion(s32[256]{0:T(256)S(1)} %compare_select_fusion.4, bf16[256,4096]{1,0:T(8,128)(2,1)} %param.5, bf16[]{:T(256)} %constant.76.clone.1), kind=kCustom, calls=%fused_computation.16 | custom fusion | bytes 3146240 | tf_op jit(solution)/shard_map/scatter | solution.py:51
  27.2 2.8 %reshape.212 = bf16[32,12,4096]{2,1,0:T(8,128)(2,1)} reshape(bf16[384,4096]{1,0:T(8,128)(2,1)S(1)} %scatter_custom_fusion.1) | data formatting | bytes 6291456 | tf_op jit(solution)/shard_map/reshape | solution.py:55
  30.0 10.0 %all-to-all-start.2 = ((bf16[32,12,4096]{2,1,0:T(8,128)(2,1)}), bf16[32,12,4096]{2,1,0:T(8,128)(2,1)}, u32[]{:S(2)}, u32[]{:S(2)}) async-start(bf16[32,12,4096]{2,1,0:T(8,128)(2,1)} %reshape.212), calls=%async_computation.2 | async-start | bytes 8388608 | tf_op jit(solution)/shard_map/all_to_all | solution.py:54
  41.0 0.7 reduce.13
  41.9 3.1 %scatter_custom_fusion.3 = s32[512]{0:T(512)S(1)} fusion(s32[384]{0:T(512)S(1)} %get-tuple-element.19, s32[384]{0:T(512)S(1)} %broadcast.287, s32[]{:T(128)} %constant.66.clone.1), kind=kCustom, calls=%fused_computation.67 | custom fusion | bytes 2052 | tf_op jit(solution)/shard_map/scatter | solution.py:76
  45.1 88.3 %all-to-all-done.2 = bf16[32,12,4096]{2,1,0:T(8,128)(2,1)} async-done(((bf16[32,12,4096]{2,1,0:T(8,128)(2,1)}), bf16[32,12,4096]{2,1,0:T(8,128)(2,1)}, u32[]{:S(2)}, u32[]{:S(2)}) %all-to-all-start.2) | async-done | bytes 3145760 | tf_op jit(solution)/shard_map/all_to_all | solution.py:54
  133.5 4.0 %reshape.260 = bf16[384,4096]{1,0:T(8,128)(2,1)S(1)} reshape(bf16[32,12,4096]{2,1,0:T(8,128)(2,1)} %all-to-all-done.2) | data formatting | bytes 6291456 | tf_op jit(solution)/shard_map/reshape | solution.py:74
  137.5 7.4 %scatter_custom_fusion.2 = bf16[512,4096]{1,0:T(8,128)(2,1)} fusion(s32[384]{0:T(512)S(1)} %get-tuple-element.19, bf16[384,4096]{1,0:T(8,128)(2,1)S(1)} %reshape.260, bf16[]{:T(256)} %constant.76.clone.1), kind=kCustom, calls=%fused_computation.13 | custom fusion | bytes 4194306 | tf_op jit(solution)/shard_map/scatter | solution.py:74
  144.8 3.2 %multiply_reduce_fusion = f32[512]{0:T(512)S(1)} fusion(bf16[512,4096]{1,0:T(8,128)(2,1)} %scatter_custom_fusion.2), kind=kLoop, calls=%fused_computation.7 | loop fusion | flops 6290944 | bytes 4196352 | tf_op jit(solution)/shard_map/reduce_sum | solution.py:19
  148.3 1.3 fusion.23
  149.6 2.8 %gather_fusion.1 = f32[384]{0:T(512)S(1)} fusion(f32[512]{0:T(512)S(1)} %select_bitcast_fusion, s32[1024]{0:T(1024)S(1)} %pad_clamp_fusion.1), kind=kCustom, calls=%fused_computation.1 | custom fusion | bytes 4608 | tf_op jit(solution)/shard_map/jit(_take)/gather | solution.py:87
  152.5 0.6 and_select_fusion.1
  153.1 8.1 %all-to-all-start.3 = ((f32[32,1,12]{2,1,0:T(1,128)}), f32[32,1,12]{2,1,0:T(1,128)S(1)}, u32[]{:S(2)}, u32[]{:S(2)}) async-start(f32[32,1,12]{2,1,0:T(1,128)} %bitcast.15), calls=%async_computation.3 | async-start | bytes 32768 | tf_op jit(solution)/shard_map/all_to_all | solution.py:90
  161.2 4.9 %gather_fusion = bf16[64,4,4096]{2,1,0:T(4,128)(2,1)S(1)} fusion(bf16[4,168,4096]{2,0,1:T(4,128)(2,1)} %all-gather.2.cloned.1.call-done, s32[1024]{0:T(1024)S(1)} %pad_clamp_fusion.2), kind=kCustom, calls=%fused_computation | custom fusion | bytes 4194560 | tf_op jit(solution)/shard_map/jit(_take)/gather | solution.py:33
  166.1 1.5 select_select_fusion
  167.7 3.6 %copy.44 = bf16[4,32,2,4096]{3,2,0,1:T(2,128)(2,1)} copy(bf16[4,32,2,4096]{3,0,2,1:T(4,128)(2,1)S(1)} %select_select_fusion) | data formatting | bytes 4194304 | tf_op jit(solution)/shard_map/jit(_where)/select_n | solution.py:34
  171.2 9.8 %all-to-all-start = ((bf16[4,32,2,4096]{3,2,0,1:T(2,128)(2,1)}), bf16[4,32,2,4096]{3,2,0,1:T(2,128)(2,1)S(1)}, u32[]{:S(2)}, u32[]{:S(2)}) async-start(bf16[4,32,2,4096]{3,2,0,1:T(2,128)(2,1)} %copy.44), calls=%async_computation | async-start | bytes 4194304 | tf_op jit(solution)/shard_map/all_to_all | solution.py:37
  181.1 2.1 multiply_reduce_fusion.2
  183.1 0.8 copy.54
  184.5 0.7 reduce.14
  185.3 1.9 gather_fusion.2
  187.3 0.6 and_select_fusion.2
  187.8 42.9 %all-to-all-done = bf16[4,32,2,4096]{3,2,0,1:T(2,128)(2,1)S(1)} async-done(((bf16[4,32,2,4096]{3,2,0,1:T(2,128)(2,1)}), bf16[4,32,2,4096]{3,2,0,1:T(2,128)(2,1)S(1)}, u32[]{:S(2)}, u32[]{:S(2)}) %all-to-all-start) | async-done | bytes 2097184 | tf_op jit(solution)/shard_map/all_to_all | solution.py:37
  230.7 2.3 multiply_reduce_fusion.1
  233.1 3.3 %fusion.18 = f32[256,2,32,4]{0,2,1,3:T(8,128)S(1)} fusion(bf16[256,4096]{1,0:T(8,128)(2,1)} %param.5, bf16[4,32,2,4096]{3,2,0,1:T(2,128)(2,1)S(1)} %all-to-all-done, f32[2,32,4]{1,0,2:T(2,128)S(1)} %copy.47, f32[256]{0:T(256)S(1)} %add_rsqrt_fusion), kind=kOutput, calls=%fused_computation.22 | convolution fusion | flops 537001984 | bytes 4458496 | tf_op jit(solution)/shard_map/nd,rpkd->nkpr/dot_general | solution.py:38
  236.6 0.8 copy.53
  (43 shorter events, 3.0 us)
Async XLA Ops:
  7.2 154.0 %all-gather.2.cloned.1.call-start = ((), (), s32[]{:S(2)}) async-start(), calls=%async_computation.4 | async-start | bytes 5734400 | tf_op jit(solution)/shard_map/all_gather | solution.py:30
  11.7 18.4 %all-to-all-start.1 = ((s32[32,1,12]{2,1,0:T(1,128)}), s32[32,1,12]{2,1,0:T(1,128)S(1)}, u32[]{:S(2)}, u32[]{:S(2)}) async-start(s32[32,1,12]{2,1,0:T(1,128)} %bitcast.9), calls=%async_computation.1 | async-start | bytes 32768 | tf_op jit(solution)/shard_map/all_to_all | solution.py:61
  30.0 10.0 %copy-start.1 = (s32[32,2]{0,1:T(2,128)S(1)}, s32[32,2]{0,1:T(2,128)}, u32[]{:S(2)}) copy-start(s32[32,2]{0,1:T(2,128)} %param.7) | copy-start | bytes 772
  30.0 103.4 %all-to-all-start.2 = ((bf16[32,12,4096]{2,1,0:T(8,128)(2,1)}), bf16[32,12,4096]{2,1,0:T(8,128)(2,1)}, u32[]{:S(2)}, u32[]{:S(2)}) async-start(bf16[32,12,4096]{2,1,0:T(8,128)(2,1)} %reshape.212), calls=%async_computation.2 | async-start | bytes 8388608 | tf_op jit(solution)/shard_map/all_to_all | solution.py:54
  144.8 3.4 %copy-start = (bf16[512,4096]{1,0:T(8,128)(2,1)S(1)}, bf16[512,4096]{1,0:T(8,128)(2,1)}, u32[]{:S(2)}) copy-start(bf16[512,4096]{1,0:T(8,128)(2,1)} %scatter_custom_fusion.2) | copy-start | bytes 12582916
  153.1 18.2 %all-to-all-start.3 = ((f32[32,1,12]{2,1,0:T(1,128)}), f32[32,1,12]{2,1,0:T(1,128)S(1)}, u32[]{:S(2)}, u32[]{:S(2)}) async-start(f32[32,1,12]{2,1,0:T(1,128)} %bitcast.15), calls=%async_computation.3 | async-start | bytes 32768 | tf_op jit(solution)/shard_map/all_to_all | solution.py:90
  171.2 59.4 %all-to-all-start = ((bf16[4,32,2,4096]{3,2,0,1:T(2,128)(2,1)}), bf16[4,32,2,4096]{3,2,0,1:T(2,128)(2,1)S(1)}, u32[]{:S(2)}, u32[]{:S(2)}) async-start(bf16[4,32,2,4096]{3,2,0,1:T(2,128)(2,1)} %copy.44), calls=%async_computation | async-start | bytes 4194304 | tf_op jit(solution)/shard_map/all_to_all | solution.py:37
Sparse Core Ops, SparseCore 0:
  10.4 60.6 all-gather.1
where the time goes:
time: 245 us; the launch traced here: 244 us
  waiting for transfers between devices  132 us (54%)
  local copies, waits for them, and re-layouts  42.2 us (17%)
  starting transfers between devices  37.9 us (15%)
  between operations  14.3 us (6%)
  other arithmetic  13.4 us (5%)
  matrix products  4.52 us (2%)
    all_to_all x1, waiting for transfers between devices, on_device(): lax.all_to_all(send_rows.reshape(shard_count, slot_count, D), 'shard', sp...  88.3 us
    all_to_all x1, waiting for transfers between devices, on_device(): lax.all_to_all(outgoing, 'shard', split_axis=1, concat_axis=1, tiled=True)  42.9 us
    all_to_all x1, starting transfers between devices, on_device(): lax.all_to_all(send_ids.reshape(shard_count, slot_count), 'shard', split_...  10.1 us
    all_to_all x1, starting transfers between devices, on_device(): lax.all_to_all(send_rows.reshape(shard_count, slot_count, D), 'shard', sp...  9.97 us
    all_to_all x1, starting transfers between devices, on_device(): lax.all_to_all(outgoing, 'shard', split_axis=1, concat_axis=1, tiled=True)  9.78 us
    all_to_all x1, starting transfers between devices, on_device(): lax.all_to_all(replies, 'shard', split_axis=0, concat_axis=0, tiled=True)  8.06 us
    reduce_sum x3, other arithmetic, inverse_norm(): mean_square = jnp.mean(jnp.square(row_data.astype(jnp.float32)), axis=-1)  7.57 us
    scatter x1, local copies, waits for them, and re-layouts, on_device(): cluster_rows = jnp.zeros((cl_dev * CAP, D), jnp.bfloat16).at[placed_at].s...  7.38 us
  transfers between devices with their start and end apart: 5, of which 2 were waited for; matrix products, arithmetic and copies ran while one was open for 21% of the time, Pallas kernels for 0%

commit v1 on v0

v1 whole, which is shorter than its diff:
```python
import functools

import jax
import jax.numpy as jnp
from jax import lax
from jax.experimental import pallas as pl
from jax.experimental.pallas import tpu as pltpu
from jax.sharding import PartitionSpec as P

D = 4096
TILE = 128
K = 2
CAP = 128
PTS = 256
CL = 4
NX, NY, NZ, NC = 4, 8, 12, 2
NS = NX * NY
NG = NZ * NC
TPG = 7
EPS = 1e-06
SCALE = 64.0
Q = 4
DQ = D // Q
DH = D // 2
MESH = pl.DeviceIdType.MESH
HI = lax.Precision.HIGHEST
F32 = jnp.float32
BF16 = jnp.bfloat16
I32 = jnp.int32
NT = (((1,), (1,)), ((), ()))


def iota(shape, dim):
    return lax.broadcasted_iota(I32, shape, dim)


def flag(cond, dtype=F32):
    return jnp.where(cond, 1.0, 0.0).astype(dtype)


def unit(total):
    return lax.rsqrt(total * (1.0 / D) + EPS) * (1.0 / 64.0)


def to_column(row):
    n = row.shape[1]
    return jnp.sum(jnp.where(iota((n, n), 0) == iota((n, n), 1), row, 0), axis=1, keepdims=True)


def to_row(column):
    n = column.shape[0]
    return jnp.sum(jnp.where(iota((n, n), 0) == iota((n, n), 1), column, 0), axis=0, keepdims=True)


def zigzag(i, n):
    return lax.rem(jnp.where(lax.rem(i, 2) == 1, (i + 1) // 2, n - i // 2), n)


def kernel(
    pts, cen, cand, asg, slt,
    out_scores, out_gram, out_best,
    send, got, tiles, csend, cgot, idsend, idgot, repsend, repgot,
    ps, pr, ids_s, ids_r, zs, zr, ks, cs, cr, rs, rr,
):
    grp, me = lax.axis_index("grp"), lax.axis_index("shard")
    z, core = grp // NC, lax.rem(grp, NC)
    x, y = me // NY, lax.rem(me, NY)

    def peer(k):
        xx = lax.rem(x + zigzag(k // NY, NX), NX)
        yy = lax.rem(y + zigzag(lax.rem(k, NY), NY), NY)
        return xx * NY + yy

    up = lax.rem(z + 1, NZ) * NC + core
    down = lax.rem(z + NZ - 1, NZ) * NC + core
    twin = z * NC + (1 - core)

    barrier = pltpu.get_barrier_semaphore()

    @pl.loop(1, NS)
    def _(k):
        pl.semaphore_signal(barrier, 1, device_id=(grp, peer(k)), device_id_type=MESH)

    for g in (up, down, twin):
        pl.semaphore_signal(barrier, 1, device_id=(g, me), device_id_type=MESH)
    pl.semaphore_wait(barrier, NS - 1 + 3)

    def tile_copy(entry, dest, ssem):
        return pltpu.make_async_remote_copy(
            src_ref=tiles.at[entry], dst_ref=tiles.at[entry], send_sem=ssem,
            recv_sem=zr.at[entry], device_id=(dest, me), device_id_type=MESH,
        )

    tiles[grp] = cen[...]
    tile_copy(grp, up, zs.at[0, 0]).start()
    tile_copy(grp, down, zs.at[1, 0]).start()
    tile_copy(grp, twin, ks.at[0, 0]).start()

    owner_row = lax.rem(asg[...] // CL, NS)
    member_row = lax.rem(asg[...], CL) * CAP + slt[...]
    own = flag(iota((NS, PTS), 0) == owner_row)
    before = flag(iota((PTS, PTS), 0) < iota((PTS, PTS), 1), BF16)
    ranks = jnp.dot(own.astype(BF16), before, preferred_element_type=F32)
    rank_row = jnp.sum(own * ranks, axis=0, keepdims=True).astype(I32)
    place_row = owner_row * 16 + rank_row
    at_rank = flag(iota((TILE, PTS), 0) == rank_row)

    ids = lax.dot_general(
        own * (member_row + 1).astype(F32), at_rank, NT, precision=HI, preferred_element_type=F32
    )
    ids = (ids + 0.5).astype(I32)
    for o in range(NS):
        idsend[o] = ids[o : o + 1]

    def quarter_slot(a, i):
        p = a * 16 + i
        quarter = (p >= 12).astype(I32) + (p >= 24).astype(I32) + (p >= 36).astype(I32)
        return quarter, p - 12 * quarter

    def point_copy(k):
        d = peer(k)
        return pltpu.make_async_remote_copy(
            src_ref=send.at[d], dst_ref=got.at[me], send_sem=ps.at[k], recv_sem=pr.at[me],
            device_id=(grp, d), device_id_type=MESH,
        )

    def id_copy(k):
        d = peer(k)
        return pltpu.make_async_remote_copy(
            src_ref=idsend.at[d], dst_ref=idgot.at[me], send_sem=ids_s.at[k], recv_sem=ids_r.at[me],
            device_id=(grp, d), device_id_type=MESH,
        )

    @pl.loop(0, NX)
    def _(j):
        xx = lax.rem(x + zigzag(j, NX), NX)
        line = iota((NY * 16, 1), 0)
        for a in range(3):
            quarter, slot = quarter_slot(a, lax.rem(line, 16))
            code = xx * (NY * 16) + line // 16 * 16 + slot
            total = None
            for q in (a, a + 1):
                pick = flag(jnp.where(quarter == q, code, -1) == place_row, BF16)
                part = jnp.dot(pick, pts[:, q * DQ : (q + 1) * DQ], preferred_element_type=F32)
                total = part if total is None else total + part
            send[pl.ds(xx * NY, NY), a * 16 : (a + 1) * 16, :] = total.astype(BF16).reshape(NY, 16, DQ)

        @pl.loop(jnp.where(j == 0, 1, 0), NY)
        def _(i):
            point_copy(j * NY + i).start()
            id_copy(j * NY + i).start()

    got[me] = send[me]
    idgot[me] = idsend[me]

    for step in range(1, NZ // 2 + 1):
        entry = lax.rem(z + NZ - step, NZ) * NC + core
        tile_copy(entry, up, zs.at[0, 0]).wait_recv()
        if step < NZ // 2:
            tile_copy(entry, up, zs.at[0, step]).start()
        tile_copy(entry, twin, ks.at[0, step]).start()
        if step < NZ // 2:
            entry = lax.rem(z + step, NZ) * NC + core
            tile_copy(entry, down, zs.at[0, 0]).wait_recv()
            if step < NZ // 2 - 1:
                tile_copy(entry, down, zs.at[1, step]).start()
            tile_copy(entry, twin, ks.at[1, step]).start()

    @pl.loop(0, NZ)
    def _(i):
        tile_copy(i * NC + 1 - core, twin, ks.at[0, 0]).wait_recv()

    line = iota((NS * 8, NS * K), 0)
    wanted = jnp.sum(
        jnp.where(line // 4 == iota((NS * 8, NS * K), 1), cand[...], 0), axis=1, keepdims=True
    )
    first = (wanted * 9363) >> 16
    code = first * 32 + lax.rem(iota((NS * 8, 1), 0), 4) * 8 + (wanted - first * TPG)
    pick = flag(code == iota((NS * 8, NG * 32), 1), BF16)

    @pl.loop(0, DH // 512)
    def _(i):
        halves = []
        for h in range(2):
            cols = pl.ds(pl.multiple_of(h * DH + i * 512, 512), 512)
            block = tiles[:, :, cols].reshape(NG * 32, 512)
            halves.append(jnp.dot(pick, block, preferred_element_type=F32).reshape(NS, 8, 512))
        both = jnp.concatenate(halves, axis=1).astype(BF16)
        csend[:, :, pl.ds(pl.multiple_of(i * 512, 512), 512)] = both

    def cen_copy(k):
        d = peer(k)
        return pltpu.make_async_remote_copy(
            src_ref=csend.at[d], dst_ref=cgot.at[me], send_sem=cs.at[k], recv_sem=cr.at[me],
            device_id=(grp, d), device_id_type=MESH,
        )

    @pl.loop(1, NS)
    def _(k):
        cen_copy(k).start()

    cgot[me] = csend[me]

    wide = pts[...].astype(F32)
    point_unit = unit(jnp.sum(wide * wide, axis=1, keepdims=True))

    def arrive(dst, sem, k):
        d = peer(k)
        pltpu.make_async_remote_copy(
            src_ref=dst.at[d], dst_ref=dst.at[d], send_sem=ps.at[0], recv_sem=sem.at[d],
            device_id=(grp, d), device_id_type=MESH,
        ).wait_recv()

    @pl.loop(1, NS)
    def _(k):
        arrive(idgot, ids_r, k)
        arrive(got, pr, k)

    idm = jnp.concatenate([idgot[o] for o in range(NS)], axis=0).astype(F32)
    lane = iota((1, NS * 16), 1)
    mine = iota((NS, NS * 16), 0) == iota((NS, NS * 16), 1) // 16

    def scatter(q, a):
        quarter, slot = quarter_slot(a, lax.rem(lane, 16))
        slot = jnp.where(quarter == q, slot, -1)
        spread = flag(iota((TILE, NS * 16), 0) == slot)
        ids = jnp.dot(idm, spread, precision=HI, preferred_element_type=F32)
        row = jnp.sum(jnp.where(mine, ids, 0.0), axis=0, keepdims=True)
        row = (row + 0.5).astype(I32)
        return iota((CL * CAP, NS * 16), 0) + 1 == row

    full = flag(scatter(0, 0))
    grams = [jnp.zeros((CAP, CAP), F32) for _ in range(CL)]
    for q in range(Q):
        maps = [(a, flag(scatter(q, a), BF16)) for a in (q - 1, q) if 0 <= a < 3]

        def step(i, acc):
            cols = pl.ds(pl.multiple_of(i * 256, 256), 256)
            rows = None
            for a, m in maps:
                block = got[:, a * 16 : (a + 1) * 16, cols].reshape(NS * 16, 256)
                part = jnp.dot(m, block, preferred_element_type=F32)
                rows = part if rows is None else rows + part
            rows = rows.astype(BF16)
            out = []
            for c in range(CL):
                r = rows[c * CAP : (c + 1) * CAP]
                out.append(acc[c] + lax.dot_general(r, r, NT, preferred_element_type=F32))
            return out

        grams = lax.fori_loop(0, DQ // 256, step, grams)

    occupied = jnp.sum(full, axis=1, keepdims=True)
    diagonal = iota((CAP, CAP), 0) == iota((CAP, CAP), 1)
    bests = []
    for c in range(CL):
        g = grams[c]
        d = jnp.where(diagonal, g, 0.0)
        u_col = unit(jnp.sum(d, axis=1, keepdims=True))
        u_row = unit(jnp.sum(d, axis=0, keepdims=True))
        g = SCALE * g * u_col * u_row
        out_gram[c] = g
        others = flag((occupied[c * CAP : (c + 1) * CAP] > 0.5) & jnp.logical_not(diagonal))
        best = jnp.max(jnp.where(others > 0.5, g, -jnp.inf), axis=0, keepdims=True)
        some = jnp.max(others, axis=0, keepdims=True) > 0.5
        bests.append(jnp.where(some, best, 0.0))
    best = jnp.concatenate(bests, axis=1)

    rep = jnp.dot(
        jnp.broadcast_to(best, (8, CL * CAP)), full, precision=HI, preferred_element_type=F32
    )[0:1]
    slots = flag(lax.rem(iota((NS * 16, TILE), 0), 16) == iota((NS * 16, TILE), 1))
    rep = jnp.dot(jnp.where(mine, rep, 0.0), slots, precision=HI, preferred_element_type=F32)
    for o in range(NS):
        repsend[o] = rep[o : o + 1]

    def rep_copy(k):
        d = peer(k)
        return pltpu.make_async_remote_copy(
            src_ref=repsend.at[d], dst_ref=repgot.at[me], send_sem=rs.at[k], recv_sem=rr.at[me],
            device_id=(grp, d), device_id_type=MESH,
        )

    @pl.loop(1, NS)
    def _(k):
        rep_copy(k).start()

    repgot[me] = repsend[me]

    @pl.loop(1, NS)
    def _(k):
        arrive(cgot, cr, k)

    line = iota((K * TILE, 1), 0)
    base = lax.rem(line, TILE) // 4 * 16 + line // TILE * 4 + lax.rem(line, 4)

    def score(i, acc):
        dots, squares = acc
        for h in range(2):
            perm = flag(base + h * 8 == iota((K * TILE, NS * 16), 1), BF16)
            block = cgot[:, :, pl.ds(pl.multiple_of(i * 512, 512), 512)].reshape(NS * 16, 512)
            rows = jnp.dot(perm, block, preferred_element_type=F32)
            squares = squares + jnp.sum(rows * rows, axis=1, keepdims=True)
            p = pts[:, pl.ds(pl.multiple_of(h * DH + i * 512, 512), 512)]
            dots = dots + lax.dot_general(p, rows.astype(BF16), NT, preferred_element_type=F32)
        return dots, squares

    dots, squares = lax.fori_loop(
        0, DH // 512, score, (jnp.zeros((PTS, K * TILE), F32), jnp.zeros((K * TILE, 1), F32))
    )
    out_scores[...] = SCALE * dots * point_unit * to_row(unit(squares))

    @pl.loop(1, NS)
    def _(k):
        arrive(repgot, rr, k)

    rep = jnp.concatenate([repgot[o] for o in range(NS)], axis=0)
    back = jnp.dot(rep, at_rank, precision=HI, preferred_element_type=F32)
    out_best[...] = jnp.sum(own * back, axis=0, keepdims=True)

    @pl.loop(1, NS)
    def _(k):
        point_copy(k).wait_send()
        id_copy(k).wait_send()
        cen_copy(k).wait_send()
        rep_copy(k).wait_send()

    tile_copy(grp, twin, ks.at[0, 0]).wait_send()
    for step in range(NZ // 2 + 1):
        if step < NZ // 2:
            tile_copy(grp, up, zs.at[0, step]).wait_send()
        if step < NZ // 2 - 1:
            tile_copy(grp, down, zs.at[1, step]).wait_send()
        if step > 0:
            tile_copy(grp, twin, ks.at[0, step]).wait_send()
        if 0 < step < NZ // 2:
            tile_copy(grp, twin, ks.at[1, step]).wait_send()


def on_device(points, centroids, candidates, assign, slot_index):
    cen = jnp.pad(centroids, ((0, 0), (0, 1), (0, 0))).reshape(4 * 8, D)
    dma = pltpu.SemaphoreType.DMA
    vmem = pl.BlockSpec(memory_space=pltpu.VMEM)
    scores, gram, best = pl.pallas_call(
        kernel,
        out_shape=(
            jax.ShapeDtypeStruct((PTS, K * TILE), F32),
            jax.ShapeDtypeStruct((CL, CAP, CAP), F32),
            jax.ShapeDtypeStruct((1, PTS), F32),
        ),
        in_specs=[vmem] * 5,
        out_specs=(vmem, vmem, vmem),
        scratch_shapes=[
            pltpu.VMEM((NS, 48, DQ), BF16),
            pltpu.VMEM((NS, 48, DQ), BF16),
            pltpu.VMEM((NG, 32, D), BF16),
            pltpu.VMEM((NS, 16, DH), BF16),
            pltpu.VMEM((NS, 16, DH), BF16),
            pltpu.VMEM((NS, 1, TILE), I32),
            pltpu.VMEM((NS, 1, TILE), I32),
            pltpu.VMEM((NS, 1, TILE), F32),
            pltpu.VMEM((NS, 1, TILE), F32),
            dma((NS,)), dma((NS,)), dma((NS,)), dma((NS,)),
            dma((2, NZ // 2)), dma((NG,)), dma((2, NZ // 2 + 1)),
            dma((NS,)), dma((NS,)), dma((NS,)), dma((NS,)),
        ],
        compiler_params=pltpu.CompilerParams(
            collective_id=0, has_side_effects=True, vmem_limit_bytes=56 << 20
        ),
        name="fused",
    )(
        points, cen, candidates.reshape(1, NS * K), assign.reshape(1, PTS),
        slot_index.reshape(1, PTS),
    )
    return scores, gram, best.reshape(PTS)


def solution(mesh):
    in_specs = (
        P(("grp", "shard"), None),
        P("shard", "grp", None),
        P("grp", None),
        P(("grp", "shard")),
        P(("grp", "shard")),
    )
    out_specs = (P(("grp", "shard"), None), P(("grp", "shard"), None, None), P(("grp", "shard")))
    return jax.shard_map(
        on_device, mesh=mesh, in_specs=in_specs, out_specs=out_specs, check_vma=False
    )
```

time: 245 us -> 156 us (0.64)
  the two profiles are of different devices: /device:TPU:656 before, /device:TPU:1 now
where the time goes in v1:
time: 156 us; the launch traced here: 153 us
  Pallas kernels  145 us (93%)
  local copies, waits for them, and re-layouts  7.73 us (5%)
    pallas_call x1, Pallas kernels, on_device(): pl.pallas_call(kernel, out_shape=(jax.ShapeDtypeStruct((PTS, K * TILE), F...  145 us
    unnamed x5, local copies, waits for them, and re-layouts  6.37 us

profile of v1, /device:TPU:1, one launch (start us, length us, event | category | flops | bytes accessed | tf_op | source)
XLA Modules:
  0.0 153.1 jit_solution(17894759519978978221)
XLA Ops:
  0.6 0.8 copy.11
  1.4 0.6 reshape.22.cand
  2.0 1.1 copy.12
  3.1 0.7 pad_bitcast_fusion.cen
  3.8 144.7 %fused.1 = (f32[256,256]{1,0:T(8,128)}, f32[4,128,128]{2,1,0:T(8,128)}, f32[1,256]{1,0:T(1,128)}) custom-call(bf16[256,4096]{1,0:T(8,128)(2,1)} %pts.1, bf16[32,4096]{1,0:T(8,128)(2,1)} %pad_bitcast_fusion.cen, s32[1,64]{1,0:T(1,128)} %reshape.22.cand, s32[1,256]{1,0:T(1,128)} %bitcast.5, s32[1,256]{1,0:T(1,128)} %bitcast.6), custom_call_target="tpu_custom_call" | custom-call | tf_op jit(solution)/shard_map/fused/pallas_call | solution.py:344
  148.6 1.7 %copy.16 = f32[256,256]{1,0:T(8,128)} copy(f32[256,256]{1,0:T(8,128)} %get-tuple-element.12) | data formatting | bytes 524288
  150.2 1.7 %copy.17 = f32[4,128,128]{2,1,0:T(8,128)} copy(f32[4,128,128]{2,1,0:T(8,128)} %get-tuple-element.13) | data formatting | bytes 524288
  151.9 1.2 copy.18

commit v2 on v1

--- a/solution.py
+++ b/solution.py
@@ -42,11 +42,6 @@
     return lax.rsqrt(total * (1.0 / D) + EPS) * (1.0 / 64.0)
 
 
-def to_column(row):
-    n = row.shape[1]
-    return jnp.sum(jnp.where(iota((n, n), 0) == iota((n, n), 1), row, 0), axis=1, keepdims=True)
-
-
 def to_row(column):
     n = column.shape[0]
     return jnp.sum(jnp.where(iota((n, n), 0) == iota((n, n), 1), column, 0), axis=0, keepdims=True)
@@ -60,7 +55,7 @@
     pts, cen, cand, asg, slt,
     out_scores, out_gram, out_best,
     send, got, tiles, csend, cgot, idsend, idgot, repsend, repgot,
-    ps, pr, ids_s, ids_r, zs, zr, ks, cs, cr, rs, rr,
+    ps, pr, ids_s, ids_r, zs, zr, ks, cs, cr, rs, rr, token,
 ):
     grp, me = lax.axis_index("grp"), lax.axis_index("shard")
     z, core = grp // NC, lax.rem(grp, NC)
@@ -74,6 +69,7 @@
     up = lax.rem(z + 1, NZ) * NC + core
     down = lax.rem(z + NZ - 1, NZ) * NC + core
     twin = z * NC + (1 - core)
+    low, high = z == 0, z == NZ - 1
 
     barrier = pltpu.get_barrier_semaphore()
 
@@ -81,9 +77,15 @@
     def _(k):
         pl.semaphore_signal(barrier, 1, device_id=(grp, peer(k)), device_id_type=MESH)
 
-    for g in (up, down, twin):
-        pl.semaphore_signal(barrier, 1, device_id=(g, me), device_id_type=MESH)
-    pl.semaphore_wait(barrier, NS - 1 + 3)
+    pl.semaphore_signal(barrier, 1, device_id=(twin, me), device_id_type=MESH)
+
+    @pl.when(jnp.logical_not(high))
+    def _():
+        pl.semaphore_signal(barrier, 1, device_id=(up, me), device_id_type=MESH)
+
+    @pl.when(jnp.logical_not(low))
+    def _():
+        pl.semaphore_signal(barrier, 1, device_id=(down, me), device_id_type=MESH)
 
     def tile_copy(entry, dest, ssem):
         return pltpu.make_async_remote_copy(
@@ -91,10 +93,8 @@
             recv_sem=zr.at[entry], device_id=(dest, me), device_id_type=MESH,
         )
 
-    tiles[grp] = cen[...]
-    tile_copy(grp, up, zs.at[0, 0]).start()
-    tile_copy(grp, down, zs.at[1, 0]).start()
-    tile_copy(grp, twin, ks.at[0, 0]).start()
+    mine = [cen[t].astype(F32) for t in range(TPG)] + [jnp.zeros((4, D), F32)]
+    tiles[grp] = jnp.concatenate(mine, axis=0).astype(BF16)
 
     owner_row = lax.rem(asg[...] // CL, NS)
     member_row = lax.rem(asg[...], CL) * CAP + slt[...]
@@ -105,13 +105,6 @@
     place_row = owner_row * 16 + rank_row
     at_rank = flag(iota((TILE, PTS), 0) == rank_row)
 
-    ids = lax.dot_general(
-        own * (member_row + 1).astype(F32), at_rank, NT, precision=HI, preferred_element_type=F32
-    )
-    ids = (ids + 0.5).astype(I32)
-    for o in range(NS):
-        idsend[o] = ids[o : o + 1]
-
     def quarter_slot(a, i):
         p = a * 16 + i
         quarter = (p >= 12).astype(I32) + (p >= 24).astype(I32) + (p >= 36).astype(I32)
@@ -131,8 +124,7 @@
             device_id=(grp, d), device_id_type=MESH,
         )
 
-    @pl.loop(0, NX)
-    def _(j):
+    def build(j):
         xx = lax.rem(x + zigzag(j, NX), NX)
         line = iota((NY * 16, 1), 0)
         for a in range(3):
@@ -145,13 +137,75 @@
                 total = part if total is None else total + part
             send[pl.ds(xx * NY, NY), a * 16 : (a + 1) * 16, :] = total.astype(BF16).reshape(NY, 16, DQ)
 
+    build(0)
+    ends = low.astype(I32) + high.astype(I32)
+    pl.semaphore_wait(barrier, NS - 1 + 3 - ends)
+
+    @pl.when(low)
+    def _():
+        pl.semaphore_signal(token.at[0], 1, device_id=(up, me), device_id_type=MESH)
+
+    @pl.when(high)
+    def _():
+        pl.semaphore_signal(token.at[1], 1, device_id=(down, me), device_id_type=MESH)
+
+    @pl.when(jnp.logical_not(high))
+    def _():
+        tile_copy(grp, up, zs.at[0, 0]).start()
+
+    @pl.when(jnp.logical_not(low))
+    def _():
+        tile_copy(grp, down, zs.at[1, 0]).start()
+
+    tile_copy(grp, twin, ks.at[0, 0]).start()
+
+    @pl.loop(0, NX)
+    def _(j):
         @pl.loop(jnp.where(j == 0, 1, 0), NY)
         def _(i):
             point_copy(j * NY + i).start()
-            id_copy(j * NY + i).start()
+
+        @pl.when(j < NX - 1)
+        def _():
+            build(j + 1)
+
+    ids = lax.dot_general(
+        own * (member_row + 1).astype(F32), at_rank, NT, precision=HI, preferred_element_type=F32
+    )
+    ids = (ids + 0.5).astype(I32)
+    for o in range(NS):
+        idsend[o] = ids[o : o + 1]
+
+    @pl.loop(1, NS)
+    def _(k):
+        id_copy(k).start()
 
     got[me] = send[me]
     idgot[me] = idsend[me]
+
+    @pl.when(jnp.logical_not(low))
+    def _():
+        pl.semaphore_wait(token.at[0], 1)
+
+        @pl.when(jnp.logical_not(high))
+        def _():
+            pl.semaphore_signal(token.at[0], 1, device_id=(up, me), device_id_type=MESH)
+
+    @pl.when(jnp.logical_not(high))
+    def _():
+        pl.semaphore_wait(token.at[1], 1)
+
+        @pl.when(jnp.logical_not(low))
+        def _():
+            pl.semaphore_signal(token.at[1], 1, device_id=(down, me), device_id_type=MESH)
+
+    @pl.when(high)
+    def _():
+        tile_copy(grp, up, zs.at[0, 0]).start()
+
+    @pl.when(low)
+    def _():
+        tile_copy(grp, down, zs.at[1, 0]).start()
 
     for step in range(1, NZ // 2 + 1):
         entry = lax.rem(z + NZ - step, NZ) * NC + core
@@ -170,12 +224,13 @@
     def _(i):
         tile_copy(i * NC + 1 - core, twin, ks.at[0, 0]).wait_recv()
 
-    line = iota((NS * 8, NS * K), 0)
-    wanted = jnp.sum(
-        jnp.where(line // 4 == iota((NS * 8, NS * K), 1), cand[...], 0), axis=1, keepdims=True
-    )
+    line = iota((NS * 8, NS), 0)
+    wanted = jnp.zeros((NS * 8, 1), I32)
+    for k in range(K):
+        here = line // 4 == iota((NS * 8, NS), 1) * K + k
+        wanted += jnp.sum(jnp.where(here, cand[k : k + 1], 0), axis=1, keepdims=True)
     first = (wanted * 9363) >> 16
-    code = first * 32 + lax.rem(iota((NS * 8, 1), 0), 4) * 8 + (wanted - first * TPG)
+    code = first * 32 + (wanted - first * TPG) * 4 + lax.rem(iota((NS * 8, 1), 0), 4)
     pick = flag(code == iota((NS * 8, NG * 32), 1), BF16)
 
     @pl.loop(0, DH // 512)
@@ -204,8 +259,7 @@
     wide = pts[...].astype(F32)
     point_unit = unit(jnp.sum(wide * wide, axis=1, keepdims=True))
 
-    def arrive(dst, sem, k):
-        d = peer(k)
+    def arrive(dst, sem, d):
         pltpu.make_async_remote_copy(
             src_ref=dst.at[d], dst_ref=dst.at[d], send_sem=ps.at[0], recv_sem=sem.at[d],
             device_id=(grp, d), device_id_type=MESH,
@@ -213,8 +267,8 @@
 
     @pl.loop(1, NS)
     def _(k):
-        arrive(idgot, ids_r, k)
-        arrive(got, pr, k)
+        arrive(idgot, ids_r, peer(k))
+        arrive(got, pr, peer(k))
 
     idm = jnp.concatenate([idgot[o] for o in range(NS)], axis=0).astype(F32)
     lane = iota((1, NS * 16), 1)
@@ -287,32 +341,41 @@
 
     repgot[me] = repsend[me]
 
-    @pl.loop(1, NS)
-    def _(k):
-        arrive(cgot, cr, k)
-
-    line = iota((K * TILE, 1), 0)
-    base = lax.rem(line, TILE) // 4 * 16 + line // TILE * 4 + lax.rem(line, 4)
-
-    def score(i, acc):
-        dots, squares = acc
-        for h in range(2):
-            perm = flag(base + h * 8 == iota((K * TILE, NS * 16), 1), BF16)
-            block = cgot[:, :, pl.ds(pl.multiple_of(i * 512, 512), 512)].reshape(NS * 16, 512)
-            rows = jnp.dot(perm, block, preferred_element_type=F32)
-            squares = squares + jnp.sum(rows * rows, axis=1, keepdims=True)
-            p = pts[:, pl.ds(pl.multiple_of(h * DH + i * 512, 512), 512)]
-            dots = dots + lax.dot_general(p, rows.astype(BF16), NT, preferred_element_type=F32)
-        return dots, squares
-
-    dots, squares = lax.fori_loop(
-        0, DH // 512, score, (jnp.zeros((PTS, K * TILE), F32), jnp.zeros((K * TILE, 1), F32))
-    )
-    out_scores[...] = SCALE * dots * point_unit * to_row(unit(squares))
-
-    @pl.loop(1, NS)
-    def _(k):
-        arrive(repgot, rr, k)
+    out_scores[...] = jnp.zeros((PTS, K * TILE), F32)
+    line = iota((NY * 8, 1), 0)
+    base = lax.rem(line, NY * 4) // 4 * 16 + line // (NY * 4) * 4 + lax.rem(line, 4)
+    column = line // (NY * 4) * TILE + lax.rem(line, NY * 4)
+
+    @pl.loop(0, NX)
+    def _(j):
+        xx = lax.rem(x - zigzag(j, NX) + NX, NX)
+
+        @pl.loop(jnp.where(j == 0, 1, 0), NY)
+        def _(i):
+            arrive(cgot, cr, xx * NY + lax.rem(y - zigzag(i, NY) + NY, NY))
+
+        def score(i, acc):
+            dots, squares = acc
+            for h in range(2):
+                perm = flag(base + h * 8 == iota((NY * 8, NY * 16), 1), BF16)
+                cols = pl.ds(pl.multiple_of(i * 512, 512), 512)
+                block = cgot[pl.ds(xx * NY, NY), :, cols].reshape(NY * 16, 512)
+                rows = jnp.dot(perm, block, preferred_element_type=F32)
+                squares = squares + jnp.sum(rows * rows, axis=1, keepdims=True)
+                p = pts[:, pl.ds(pl.multiple_of(h * DH + i * 512, 512), 512)]
+                dots = dots + lax.dot_general(p, rows.astype(BF16), NT, preferred_element_type=F32)
+            return dots, squares
+
+        dots, squares = lax.fori_loop(
+            0, DH // 512, score, (jnp.zeros((PTS, NY * 8), F32), jnp.zeros((NY * 8, 1), F32))
+        )
+        put = flag(column + xx * (NY * 4) == iota((NY * 8, K * TILE), 1))
+        dots = SCALE * dots * point_unit * to_row(unit(squares))
+        out_scores[...] += jnp.dot(dots, put, precision=HI, preferred_element_type=F32)
+
+    @pl.loop(1, NS)
+    def _(k):
+        arrive(repgot, rr, peer(k))
 
     rep = jnp.concatenate([repgot[o] for o in range(NS)], axis=0)
     back = jnp.dot(rep, at_rank, precision=HI, preferred_element_type=F32)
@@ -337,11 +400,17 @@
             tile_copy(grp, twin, ks.at[1, step]).wait_send()
 
 
+def deliver(a, b, c, out_a, out_b, out_c):
+    out_a[...] = a[...]
+    out_b[...] = b[...]
+    out_c[...] = c[...]
+
+
 def on_device(points, centroids, candidates, assign, slot_index):
-    cen = jnp.pad(centroids, ((0, 0), (0, 1), (0, 0))).reshape(4 * 8, D)
+    cen = jnp.transpose(centroids, (1, 0, 2))
     dma = pltpu.SemaphoreType.DMA
     vmem = pl.BlockSpec(memory_space=pltpu.VMEM)
-    scores, gram, best = pl.pallas_call(
+    outs = pl.pallas_call(
         kernel,
         out_shape=(
             jax.ShapeDtypeStruct((PTS, K * TILE), F32),
@@ -363,15 +432,24 @@
             dma((NS,)), dma((NS,)), dma((NS,)), dma((NS,)),
             dma((2, NZ // 2)), dma((NG,)), dma((2, NZ // 2 + 1)),
             dma((NS,)), dma((NS,)), dma((NS,)), dma((NS,)),
+            pltpu.SemaphoreType.REGULAR((2,)),
         ],
         compiler_params=pltpu.CompilerParams(
             collective_id=0, has_side_effects=True, vmem_limit_bytes=56 << 20
         ),
         name="fused",
     )(
-        points, cen, candidates.reshape(1, NS * K), assign.reshape(1, PTS),
+        points, cen, candidates.T, assign.reshape(1, PTS),
         slot_index.reshape(1, PTS),
     )
+    scores, gram, best = pl.pallas_call(
+        deliver,
+        out_shape=tuple(jax.ShapeDtypeStruct(o.shape, o.dtype) for o in outs),
+        in_specs=[vmem] * 3,
+        out_specs=(vmem,) * 3,
+        compiler_params=pltpu.CompilerParams(vmem_limit_bytes=56 << 20),
+        name="deliver",
+    )(*outs)
     return scores, gram, best.reshape(PTS)
 
 

time: 156 us -> 140 us (0.90); the launches traced: 153 us -> 139 us
  local copies, waits for them, and re-layouts: 7.73 us -> 0 us
  Pallas kernels: 145 us -> 138 us
    pallas_call x1, Pallas kernels: 145 us -> 136 us  [on_device(): pl.pallas_call(kernel, out_shape=(jax.ShapeDtypeStruct((PTS, K * TILE), F...]
    unnamed x5 -> x0, local copies, waits for them, and re-layouts: 6.37 us -> none
    pallas_call x0 -> x1, Pallas kernels: none -> 1.84 us  [on_device(): pl.pallas_call(deliver, out_shape=tuple((jax.ShapeDtypeStruct(o.shape, o....]
where the time goes in v2:
time: 140 us; the launch traced here: 139 us
  Pallas kernels  138 us (99%)
    pallas_call x1, Pallas kernels, on_device(): pl.pallas_call(kernel, out_shape=(jax.ShapeDtypeStruct((PTS, K * TILE), F...  136 us

profile of v2, /device:TPU:1, one launch (start us, length us, event | category | flops | bytes accessed | tf_op | source)
XLA Modules:
  0.0 139.0 jit_solution(4886249546969928330)
XLA Ops:
  0.6 136.5 %fused.1 = (f32[256,256]{1,0:T(8,128)}, f32[4,128,128]{2,1,0:T(8,128)}, f32[1,256]{1,0:T(1,128)}) custom-call(bf16[256,4096]{1,0:T(8,128)(2,1)} %pts.1, bf16[7,4,4096]{2,1,0:T(4,128)(2,1)} %bitcast.5, s32[2,32]{1,0:T(2,128)} %bitcast.6, s32[1,256]{1,0:T(1,128)} %bitcast.7, s32[1,256]{1,0:T(1,128)} %bitcast.8), custom_call_target="tpu_custom_call" | custom-call | tf_op jit(solution)/shard_map/fused/pallas_call | solution.py:413
  137.1 1.8 %deliver.1 = (f32[256,256]{1,0:T(8,128)}, f32[4,128,128]{2,1,0:T(8,128)}, f32[1,256]{1,0:T(1,128)}) custom-call(f32[256,256]{1,0:T(8,128)} %get-tuple-element.9.a, f32[4,128,128]{2,1,0:T(8,128)} %get-tuple-element.10.b, f32[1,256]{1,0:T(1,128)} %get-tuple-element.11.c), custom_call_target="tpu_custom_call" | custom-call | tf_op jit(solution)/shard_map/deliver/pallas_call | solution.py:445

commit v3 on v2

--- a/solution.py
+++ b/solution.py
@@ -55,7 +55,7 @@
     pts, cen, cand, asg, slt,
     out_scores, out_gram, out_best,
     send, got, tiles, csend, cgot, idsend, idgot, repsend, repgot,
-    ps, pr, ids_s, ids_r, zs, zr, ks, cs, cr, rs, rr, token,
+    ps, pr, ids_s, ids_r, zs, zr, ks, cs, cr, rs, rr, token, xs,
 ):
     grp, me = lax.axis_index("grp"), lax.axis_index("shard")
     z, core = grp // NC, lax.rem(grp, NC)
@@ -87,14 +87,21 @@
     def _():
         pl.semaphore_signal(barrier, 1, device_id=(down, me), device_id_type=MESH)
 
-    def tile_copy(entry, dest, ssem):
+    across = x * NY + lax.rem(y + NY // 2, NY)
+
+    def tile_copy(part, entry, dest, ssem):
         return pltpu.make_async_remote_copy(
-            src_ref=tiles.at[entry], dst_ref=tiles.at[entry], send_sem=ssem,
-            recv_sem=zr.at[entry], device_id=(dest, me), device_id_type=MESH,
+            src_ref=tiles.at[part, entry], dst_ref=tiles.at[part, entry], send_sem=ssem,
+            recv_sem=zr.at[part, entry], device_id=(dest, me), device_id_type=MESH,
         )
 
+    swap = pltpu.make_async_remote_copy(
+        src_ref=tiles.at[0, grp], dst_ref=tiles.at[1, grp], send_sem=xs.at[0],
+        recv_sem=zr.at[1, grp], device_id=(grp, across), device_id_type=MESH,
+    )
+
     mine = [cen[t].astype(F32) for t in range(TPG)] + [jnp.zeros((4, D), F32)]
-    tiles[grp] = jnp.concatenate(mine, axis=0).astype(BF16)
+    tiles[0, grp] = jnp.concatenate(mine, axis=0).astype(BF16)
 
     owner_row = lax.rem(asg[...] // CL, NS)
     member_row = lax.rem(asg[...], CL) * CAP + slt[...]
@@ -149,15 +156,20 @@
     def _():
         pl.semaphore_signal(token.at[1], 1, device_id=(down, me), device_id_type=MESH)
 
-    @pl.when(jnp.logical_not(high))
-    def _():
-        tile_copy(grp, up, zs.at[0, 0]).start()
-
-    @pl.when(jnp.logical_not(low))
-    def _():
-        tile_copy(grp, down, zs.at[1, 0]).start()
-
-    tile_copy(grp, twin, ks.at[0, 0]).start()
+    swap.start()
+
+    def own_tiles(part):
+        @pl.when(jnp.logical_not(high))
+        def _():
+            tile_copy(part, grp, up, zs.at[part, 0, 0]).start()
+
+        @pl.when(jnp.logical_not(low))
+        def _():
+            tile_copy(part, grp, down, zs.at[part, 1, 0]).start()
+
+        tile_copy(part, grp, twin, ks.at[part, 0, 0]).start()
+
+    own_tiles(0)
 
     @pl.loop(0, NX)
     def _(j):
@@ -183,6 +195,13 @@
     got[me] = send[me]
     idgot[me] = idsend[me]
 
+    def token_down():
+        pl.semaphore_wait(token.at[1], 1)
+
+        @pl.when(jnp.logical_not(low))
+        def _():
+            pl.semaphore_signal(token.at[1], 1, device_id=(down, me), device_id_type=MESH)
+
     @pl.when(jnp.logical_not(low))
     def _():
         pl.semaphore_wait(token.at[0], 1)
@@ -191,70 +210,119 @@
         def _():
             pl.semaphore_signal(token.at[0], 1, device_id=(up, me), device_id_type=MESH)
 
-    @pl.when(jnp.logical_not(high))
-    def _():
-        pl.semaphore_wait(token.at[1], 1)
-
-        @pl.when(jnp.logical_not(low))
-        def _():
-            pl.semaphore_signal(token.at[1], 1, device_id=(down, me), device_id_type=MESH)
+    @pl.when((z >= NZ // 2) & (z < NZ - 1))
+    def _():
+        token_down()
 
     @pl.when(high)
     def _():
-        tile_copy(grp, up, zs.at[0, 0]).start()
-
-    @pl.when(low)
-    def _():
-        tile_copy(grp, down, zs.at[1, 0]).start()
-
-    for step in range(1, NZ // 2 + 1):
-        entry = lax.rem(z + NZ - step, NZ) * NC + core
-        tile_copy(entry, up, zs.at[0, 0]).wait_recv()
-        if step < NZ // 2:
-            tile_copy(entry, up, zs.at[0, step]).start()
-        tile_copy(entry, twin, ks.at[0, step]).start()
-        if step < NZ // 2:
-            entry = lax.rem(z + step, NZ) * NC + core
-            tile_copy(entry, down, zs.at[0, 0]).wait_recv()
-            if step < NZ // 2 - 1:
-                tile_copy(entry, down, zs.at[1, step]).start()
-            tile_copy(entry, twin, ks.at[1, step]).start()
-
-    @pl.loop(0, NZ)
-    def _(i):
-        tile_copy(i * NC + 1 - core, twin, ks.at[0, 0]).wait_recv()
-
-    line = iota((NS * 8, NS), 0)
-    wanted = jnp.zeros((NS * 8, 1), I32)
-    for k in range(K):
-        here = line // 4 == iota((NS * 8, NS), 1) * K + k
-        wanted += jnp.sum(jnp.where(here, cand[k : k + 1], 0), axis=1, keepdims=True)
-    first = (wanted * 9363) >> 16
-    code = first * 32 + (wanted - first * TPG) * 4 + lax.rem(iota((NS * 8, 1), 0), 4)
-    pick = flag(code == iota((NS * 8, NG * 32), 1), BF16)
-
-    @pl.loop(0, DH // 512)
-    def _(i):
-        halves = []
-        for h in range(2):
-            cols = pl.ds(pl.multiple_of(h * DH + i * 512, 512), 512)
-            block = tiles[:, :, cols].reshape(NG * 32, 512)
-            halves.append(jnp.dot(pick, block, preferred_element_type=F32).reshape(NS, 8, 512))
-        both = jnp.concatenate(halves, axis=1).astype(BF16)
-        csend[:, :, pl.ds(pl.multiple_of(i * 512, 512), 512)] = both
-
-    def cen_copy(k):
-        d = peer(k)
+        tile_copy(0, grp, up, zs.at[0, 0, 0]).start()
+
+    reach = ((NZ // 2, NZ // 2 - 1), (NZ // 2 - 1, NZ // 2))
+
+    def forward(part, way, step):
+        dest, shift = ((up, NZ - step), (down, step))[way]
+        entry = lax.rem(z + shift, NZ) * NC + core
+        tile_copy(part, entry, dest, zs.at[part, way, 0]).wait_recv()
+
+        @pl.when(step < reach[part][way])
+        def _():
+            tile_copy(part, entry, dest, zs.at[part, way, step]).start()
+
+        tile_copy(part, entry, twin, ks.at[part, way, step]).start()
+
+    lags = ((0, 3), (2, 6))
+
+    def turn(t):
+        for part in range(2):
+            for late in range(2):
+                for way in range(2):
+                    step = t - lags[part][late]
+                    if (part, late, way) == (0, 0, 1):
+                        step -= low.astype(I32)
+                    inside = (z, NZ - 1 - z)[way]
+                    due = step > inside if late else step <= inside
+
+                    @pl.when(due & (step >= 1) & (step <= reach[part][way]))
+                    def _():
+                        forward(part, way, step)
+
+    def near(i, count):
+        xx = lax.rem(x + zigzag(i // count, NX), NX)
+        return xx * NY + lax.rem(y + zigzag(lax.rem(i, count), NY), NY)
+
+    def cen_copy(part, i):
+        slot = (me, across)[part]
+        d = near(i, (5, 3)[part])
+        j = i + (0, 5 * NX)[part]
         return pltpu.make_async_remote_copy(
-            src_ref=csend.at[d], dst_ref=cgot.at[me], send_sem=cs.at[k], recv_sem=cr.at[me],
+            src_ref=csend.at[j], dst_ref=cgot.at[slot], send_sem=cs.at[j], recv_sem=cr.at[slot],
             device_id=(grp, d), device_id_type=MESH,
         )
 
-    @pl.loop(1, NS)
-    def _(k):
-        cen_copy(k).start()
-
-    cgot[me] = csend[me]
+    def select(part):
+        @pl.loop(0, NZ)
+        def _(i):
+            tile_copy(part, i * NC + 1 - core, twin, ks.at[part, 0, 0]).wait_recv()
+
+        count = (5, 3)[part]
+        n = count * NX
+        line = iota((n * 8, NS), 0)
+        dest = near(line // 8, count) == iota((n * 8, NS), 1)
+        wanted = jnp.zeros((n * 8, 1), I32)
+        for k in range(K):
+            here = dest & (lax.rem(line, 8) // 4 == k)
+            wanted += jnp.sum(jnp.where(here, cand[k : k + 1], 0), axis=1, keepdims=True)
+        first = (wanted * 9363) >> 16
+        code = first * 32 + (wanted - first * TPG) * 4 + lax.rem(iota((n * 8, 1), 0), 4)
+        pick = flag(code == iota((n * 8, NG * 32), 1), BF16)
+        start = (0, 5 * NX)[part]
+
+        @pl.loop(0, DH // 512)
+        def _(i):
+            halves = []
+            for h in range(2):
+                cols = pl.ds(pl.multiple_of(h * DH + i * 512, 512), 512)
+                block = tiles[part, :, :, cols].reshape(NG * 32, 512)
+                halves.append(jnp.dot(pick, block, preferred_element_type=F32).reshape(n, 8, 512))
+            both = jnp.concatenate(halves, axis=1).astype(BF16)
+            csend[start : start + n, :, pl.ds(pl.multiple_of(i * 512, 512), 512)] = both
+
+        @pl.loop(1, n)
+        def _(i):
+            cen_copy(part, i).start()
+
+        cgot[(me, across)[part]] = csend[start]
+
+    @pl.loop(1, 10)
+    def _(t):
+        turn(t)
+
+        @pl.when(t == 1)
+        def _():
+            swap.wait_recv()
+            own_tiles(1)
+
+            @pl.when(high)
+            def _():
+                tile_copy(1, grp, up, zs.at[1, 0, 0]).start()
+
+            @pl.when(z < NZ // 2)
+            def _():
+                token_down()
+
+            @pl.when(low)
+            def _():
+                for part in range(2):
+                    tile_copy(part, grp, down, zs.at[part, 1, 0]).start()
+
+    select(0)
+
+    @pl.loop(10, 13)
+    def _(t):
+        turn(t)
+
+    select(1)
 
     wide = pts[...].astype(F32)
     point_unit = unit(jnp.sum(wide * wide, axis=1, keepdims=True))
@@ -350,7 +418,7 @@
     def _(j):
         xx = lax.rem(x - zigzag(j, NX) + NX, NX)
 
-        @pl.loop(jnp.where(j == 0, 1, 0), NY)
+        @pl.loop(jnp.where(j == 0, 1, 0), jnp.where(j == 0, NY - 1, NY))
         def _(i):
             arrive(cgot, cr, xx * NY + lax.rem(y - zigzag(i, NY) + NY, NY))
 
@@ -385,19 +453,20 @@
     def _(k):
         point_copy(k).wait_send()
         id_copy(k).wait_send()
-        cen_copy(k).wait_send()
         rep_copy(k).wait_send()
 
-    tile_copy(grp, twin, ks.at[0, 0]).wait_send()
-    for step in range(NZ // 2 + 1):
-        if step < NZ // 2:
-            tile_copy(grp, up, zs.at[0, step]).wait_send()
-        if step < NZ // 2 - 1:
-            tile_copy(grp, down, zs.at[1, step]).wait_send()
-        if step > 0:
-            tile_copy(grp, twin, ks.at[0, step]).wait_send()
-        if 0 < step < NZ // 2:
-            tile_copy(grp, twin, ks.at[1, step]).wait_send()
+    swap.wait_send()
+    for part in range(2):
+
+        @pl.loop(1, (5, 3)[part] * NX)
+        def _(i):
+            cen_copy(part, i).wait_send()
+
+        tile_copy(part, grp, twin, ks.at[part, 0, 0]).wait_send()
+        for way in range(2):
+            for step in range(reach[part][way]):
+                tile_copy(part, grp, up, zs.at[part, way, step]).wait_send()
+                tile_copy(part, grp, twin, ks.at[part, way, step + 1]).wait_send()
 
 
 def deliver(a, b, c, out_a, out_b, out_c):
@@ -422,7 +491,7 @@
         scratch_shapes=[
             pltpu.VMEM((NS, 48, DQ), BF16),
             pltpu.VMEM((NS, 48, DQ), BF16),
-            pltpu.VMEM((NG, 32, D), BF16),
+            pltpu.VMEM((2, NG, 32, D), BF16),
             pltpu.VMEM((NS, 16, DH), BF16),
             pltpu.VMEM((NS, 16, DH), BF16),
             pltpu.VMEM((NS, 1, TILE), I32),
@@ -430,9 +499,9 @@
             pltpu.VMEM((NS, 1, TILE), F32),
             pltpu.VMEM((NS, 1, TILE), F32),
             dma((NS,)), dma((NS,)), dma((NS,)), dma((NS,)),
-            dma((2, NZ // 2)), dma((NG,)), dma((2, NZ // 2 + 1)),
+            dma((2, 2, NZ // 2)), dma((2, NG)), dma((2, 2, NZ // 2 + 1)),
             dma((NS,)), dma((NS,)), dma((NS,)), dma((NS,)),
-            pltpu.SemaphoreType.REGULAR((2,)),
+            pltpu.SemaphoreType.REGULAR((2,)), dma((1,)),
         ],
         compiler_params=pltpu.CompilerParams(
             collective_id=0, has_side_effects=True, vmem_limit_bytes=56 << 20

time: 140 us -> 157 us (1.12)
  the two profiles are of different devices: /device:TPU:1 before, /device:TPU:393 now
where the time goes in v3:
time: 157 us
  Pallas kernels  156 us (99%)
    pallas_call x1, Pallas kernels, on_device(): pl.pallas_call(kernel, out_shape=(jax.ShapeDtypeStruct((PTS, K * TILE), F...  155 us

profile of v3, /device:TPU:393, one launch (start us, length us, event | category | flops | bytes accessed | tf_op | source)
XLA Modules:
  0.0 157.1 jit_solution(6360011839918477838)
XLA Ops:
  0.6 154.6 %fused.1 = (f32[256,256]{1,0:T(8,128)}, f32[4,128,128]{2,1,0:T(8,128)}, f32[1,256]{1,0:T(1,128)}) custom-call(bf16[256,4096]{1,0:T(8,128)(2,1)} %pts.1, bf16[7,4,4096]{2,1,0:T(4,128)(2,1)} %bitcast.5, s32[2,32]{1,0:T(2,128)} %bitcast.6, s32[1,256]{1,0:T(1,128)} %bitcast.7, s32[1,256]{1,0:T(1,128)} %bitcast.8), custom_call_target="tpu_custom_call" | custom-call | tf_op jit(solution)/shard_map/fused/pallas_call | solution.py:482
  155.3 1.8 %deliver.1 = (f32[256,256]{1,0:T(8,128)}, f32[4,128,128]{2,1,0:T(8,128)}, f32[1,256]{1,0:T(1,128)}) custom-call(f32[256,256]{1,0:T(8,128)} %get-tuple-element.9.a, f32[4,128,128]{2,1,0:T(8,128)} %get-tuple-element.10.b, f32[1,256]{1,0:T(1,128)} %get-tuple-element.11.c), custom_call_target="tpu_custom_call" | custom-call | tf_op jit(solution)/shard_map/deliver/pallas_call | solution.py:514

commit v4 on v2

--- a/solution.py
+++ b/solution.py
@@ -52,11 +52,13 @@
 
 
 def kernel(
-    pts, cen, cand, asg, slt,
+    pts_hbm, cen, cand, asg, slt,
     out_scores, out_gram, out_best,
     send, got, tiles, csend, cgot, idsend, idgot, repsend, repgot,
-    ps, pr, ids_s, ids_r, zs, zr, ks, cs, cr, rs, rr, token,
+    ps, pr, ids_s, ids_r, zs, zr, ks, cs, cr, rs, rr, token, pts, fs,
 ):
+    fetch = pltpu.make_async_copy(pts_hbm, pts, fs.at[0])
+    fetch.start()
     grp, me = lax.axis_index("grp"), lax.axis_index("shard")
     z, core = grp // NC, lax.rem(grp, NC)
     x, y = me // NY, lax.rem(me, NY)
@@ -92,9 +94,6 @@
             src_ref=tiles.at[entry], dst_ref=tiles.at[entry], send_sem=ssem,
             recv_sem=zr.at[entry], device_id=(dest, me), device_id_type=MESH,
         )
-
-    mine = [cen[t].astype(F32) for t in range(TPG)] + [jnp.zeros((4, D), F32)]
-    tiles[grp] = jnp.concatenate(mine, axis=0).astype(BF16)
 
     owner_row = lax.rem(asg[...] // CL, NS)
     member_row = lax.rem(asg[...], CL) * CAP + slt[...]
@@ -137,6 +136,7 @@
                 total = part if total is None else total + part
             send[pl.ds(xx * NY, NY), a * 16 : (a + 1) * 16, :] = total.astype(BF16).reshape(NY, 16, DQ)
 
+    fetch.wait()
     build(0)
     ends = low.astype(I32) + high.astype(I32)
     pl.semaphore_wait(barrier, NS - 1 + 3 - ends)
@@ -149,25 +149,29 @@
     def _():
         pl.semaphore_signal(token.at[1], 1, device_id=(down, me), device_id_type=MESH)
 
-    @pl.when(jnp.logical_not(high))
-    def _():
-        tile_copy(grp, up, zs.at[0, 0]).start()
-
-    @pl.when(jnp.logical_not(low))
-    def _():
-        tile_copy(grp, down, zs.at[1, 0]).start()
-
-    tile_copy(grp, twin, ks.at[0, 0]).start()
-
-    @pl.loop(0, NX)
-    def _(j):
+    def send_points(j):
         @pl.loop(jnp.where(j == 0, 1, 0), NY)
         def _(i):
             point_copy(j * NY + i).start()
 
-        @pl.when(j < NX - 1)
-        def _():
-            build(j + 1)
+    send_points(0)
+    mine = [cen[t].astype(F32) for t in range(TPG)] + [jnp.zeros((4, D), F32)]
+    tiles[grp] = jnp.concatenate(mine, axis=0).astype(BF16)
+
+    @pl.when(jnp.logical_not(high))
+    def _():
+        tile_copy(grp, up, zs.at[0, 0]).start()
+
+    @pl.when(jnp.logical_not(low))
+    def _():
+        tile_copy(grp, down, zs.at[1, 0]).start()
+
+    tile_copy(grp, twin, ks.at[0, 0]).start()
+
+    @pl.loop(1, NX)
+    def _(j):
+        build(j)
+        send_points(j)
 
     ids = lax.dot_general(
         own * (member_row + 1).astype(F32), at_rank, NT, precision=HI, preferred_element_type=F32
@@ -183,6 +187,13 @@
     got[me] = send[me]
     idgot[me] = idsend[me]
 
+    def token_down():
+        pl.semaphore_wait(token.at[1], 1)
+
+        @pl.when(jnp.logical_not(low))
+        def _():
+            pl.semaphore_signal(token.at[1], 1, device_id=(down, me), device_id_type=MESH)
+
     @pl.when(jnp.logical_not(low))
     def _():
         pl.semaphore_wait(token.at[0], 1)
@@ -191,34 +202,48 @@
         def _():
             pl.semaphore_signal(token.at[0], 1, device_id=(up, me), device_id_type=MESH)
 
-    @pl.when(jnp.logical_not(high))
-    def _():
-        pl.semaphore_wait(token.at[1], 1)
-
-        @pl.when(jnp.logical_not(low))
+    @pl.when((z >= NZ // 2) & (z < NZ - 1))
+    def _():
+        token_down()
+
+    @pl.when(high)
+    def _():
+        tile_copy(grp, up, zs.at[0, 0]).start()
+
+    reach = (NZ // 2, NZ // 2 - 1)
+
+    def forward(way, step):
+        dest, shift = ((up, NZ - step), (down, step))[way]
+        entry = lax.rem(z + shift, NZ) * NC + core
+        tile_copy(entry, dest, zs.at[way, 0]).wait_recv()
+
+        @pl.when(step < reach[way])
         def _():
-            pl.semaphore_signal(token.at[1], 1, device_id=(down, me), device_id_type=MESH)
-
-    @pl.when(high)
-    def _():
-        tile_copy(grp, up, zs.at[0, 0]).start()
-
-    @pl.when(low)
-    def _():
-        tile_copy(grp, down, zs.at[1, 0]).start()
-
-    for step in range(1, NZ // 2 + 1):
-        entry = lax.rem(z + NZ - step, NZ) * NC + core
-        tile_copy(entry, up, zs.at[0, 0]).wait_recv()
-        if step < NZ // 2:
-            tile_copy(entry, up, zs.at[0, step]).start()
-        tile_copy(entry, twin, ks.at[0, step]).start()
-        if step < NZ // 2:
-            entry = lax.rem(z + step, NZ) * NC + core
-            tile_copy(entry, down, zs.at[0, 0]).wait_recv()
-            if step < NZ // 2 - 1:
-                tile_copy(entry, down, zs.at[1, step]).start()
-            tile_copy(entry, twin, ks.at[1, step]).start()
+            tile_copy(entry, dest, zs.at[way, step]).start()
+
+        tile_copy(entry, twin, ks.at[way, step]).start()
+
+    @pl.loop(1, NZ // 2 + 4)
+    def _(t):
+        for late in range(2):
+            for way in range(2):
+                step = t - 3 * late
+                if (late, way) == (0, 1):
+                    step -= low.astype(I32)
+                inside = (z, NZ - 1 - z)[way]
+                due = step > inside if late else step <= inside
+
+                @pl.when(due & (step >= 1) & (step <= reach[way]))
+                def _():
+                    forward(way, step)
+
+        @pl.when((t == 1) & (z < NZ // 2))
+        def _():
+            token_down()
+
+        @pl.when((t == 1) & low)
+        def _():
+            tile_copy(grp, down, zs.at[1, 0]).start()
 
     @pl.loop(0, NZ)
     def _(i):
@@ -341,13 +366,23 @@
 
     repgot[me] = repsend[me]
 
+    @pl.loop(1, NS)
+    def _(k):
+        point_copy(k).wait_send()
+        id_copy(k).wait_send()
+
+    tile_copy(grp, twin, ks.at[0, 0]).wait_send()
+    for way in range(2):
+        for step in range(reach[way]):
+            tile_copy(grp, up, zs.at[way, step]).wait_send()
+            tile_copy(grp, twin, ks.at[way, step + 1]).wait_send()
+
     out_scores[...] = jnp.zeros((PTS, K * TILE), F32)
     line = iota((NY * 8, 1), 0)
     base = lax.rem(line, NY * 4) // 4 * 16 + line // (NY * 4) * 4 + lax.rem(line, 4)
     column = line // (NY * 4) * TILE + lax.rem(line, NY * 4)
 
-    @pl.loop(0, NX)
-    def _(j):
+    def column_scores(j):
         xx = lax.rem(x - zigzag(j, NX) + NX, NX)
 
         @pl.loop(jnp.where(j == 0, 1, 0), NY)
@@ -373,6 +408,14 @@
         dots = SCALE * dots * point_unit * to_row(unit(squares))
         out_scores[...] += jnp.dot(dots, put, precision=HI, preferred_element_type=F32)
 
+        @pl.loop(jnp.where(j == 0, 1, 0), NY)
+        def _(i):
+            cen_copy(j * NY + i).wait_send()
+
+    @pl.loop(0, NX - 1)
+    def _(j):
+        column_scores(j)
+
     @pl.loop(1, NS)
     def _(k):
         arrive(repgot, rr, peer(k))
@@ -383,21 +426,9 @@
 
     @pl.loop(1, NS)
     def _(k):
-        point_copy(k).wait_send()
-        id_copy(k).wait_send()
-        cen_copy(k).wait_send()
         rep_copy(k).wait_send()
 
-    tile_copy(grp, twin, ks.at[0, 0]).wait_send()
-    for step in range(NZ // 2 + 1):
-        if step < NZ // 2:
-            tile_copy(grp, up, zs.at[0, step]).wait_send()
-        if step < NZ // 2 - 1:
-            tile_copy(grp, down, zs.at[1, step]).wait_send()
-        if step > 0:
-            tile_copy(grp, twin, ks.at[0, step]).wait_send()
-        if 0 < step < NZ // 2:
-            tile_copy(grp, twin, ks.at[1, step]).wait_send()
+    column_scores(NX - 1)
 
 
 def deliver(a, b, c, out_a, out_b, out_c):
@@ -417,7 +448,7 @@
             jax.ShapeDtypeStruct((CL, CAP, CAP), F32),
             jax.ShapeDtypeStruct((1, PTS), F32),
         ),
-        in_specs=[vmem] * 5,
+        in_specs=[pl.BlockSpec(memory_space=pl.ANY)] + [vmem] * 4,
         out_specs=(vmem, vmem, vmem),
         scratch_shapes=[
             pltpu.VMEM((NS, 48, DQ), BF16),
@@ -433,6 +464,7 @@
             dma((2, NZ // 2)), dma((NG,)), dma((2, NZ // 2 + 1)),
             dma((NS,)), dma((NS,)), dma((NS,)), dma((NS,)),
             pltpu.SemaphoreType.REGULAR((2,)),
+            pltpu.VMEM((PTS, D), BF16), dma((1,)),
         ],
         compiler_params=pltpu.CompilerParams(
             collective_id=0, has_side_effects=True, vmem_limit_bytes=56 << 20

time: 140 us -> 140 us (level)
  the two profiles are of different devices: /device:TPU:1 before, /device:TPU:209 now
where the time goes in v4:
time: 140 us; the launch traced here: 139 us
  Pallas kernels  139 us (99%)
    pallas_call x1, Pallas kernels, on_device(): pl.pallas_call(kernel, out_shape=(jax.ShapeDtypeStruct((PTS, K * TILE), F...  137 us

profile of v4, /device:TPU:209, one launch (start us, length us, event | category | flops | bytes accessed | tf_op | source)
XLA Modules:
  0.0 139.4 jit_solution(10443319900958475954)
XLA Ops:
  0.6 136.9 %fused.1 = (f32[256,256]{1,0:T(8,128)}, f32[4,128,128]{2,1,0:T(8,128)}, f32[1,256]{1,0:T(1,128)}) custom-call(bf16[256,4096]{1,0:T(8,128)(2,1)} %pts_hbm.1, bf16[7,4,4096]{2,1,0:T(4,128)(2,1)} %bitcast.5, s32[2,32]{1,0:T(2,128)} %bitcast.6, s32[1,256]{1,0:T(1,128)} %bitcast.7, s32[1,256]{1,0:T(1,128)} %bitcast.8), custom_call_target="tpu_custom_call" | custom-call | tf_op jit(solution)/shard_map/fused/pallas_call | solution.py:444
  137.5 1.8 %deliver.1 = (f32[256,256]{1,0:T(8,128)}, f32[4,128,128]{2,1,0:T(8,128)}, f32[1,256]{1,0:T(1,128)}) custom-call(f32[256,256]{1,0:T(8,128)} %get-tuple-element.9.a, f32[4,128,128]{2,1,0:T(8,128)} %get-tuple-element.10.b, f32[1,256]{1,0:T(1,128)} %get-tuple-element.11.c), custom_call_target="tpu_custom_call" | custom-call | tf_op jit(solution)/shard_map/deliver/pallas_call | solution.py:477

commit v5 on v4

--- a/solution.py
+++ b/solution.py
@@ -155,12 +155,30 @@
             point_copy(j * NY + i).start()
 
     send_points(0)
+
+    def token_down():
+        pl.semaphore_wait(token.at[1], 1)
+
+        @pl.when(jnp.logical_not(low))
+        def _():
+            pl.semaphore_signal(token.at[1], 1, device_id=(down, me), device_id_type=MESH)
+
+    @pl.when(jnp.logical_not(low))
+    def _():
+        pl.semaphore_wait(token.at[0], 1)
+
+        @pl.when(jnp.logical_not(high))
+        def _():
+            pl.semaphore_signal(token.at[0], 1, device_id=(up, me), device_id_type=MESH)
+
+    @pl.when((z >= NZ // 2) & (z < NZ - 1))
+    def _():
+        token_down()
+
     mine = [cen[t].astype(F32) for t in range(TPG)] + [jnp.zeros((4, D), F32)]
     tiles[grp] = jnp.concatenate(mine, axis=0).astype(BF16)
 
-    @pl.when(jnp.logical_not(high))
-    def _():
-        tile_copy(grp, up, zs.at[0, 0]).start()
+    tile_copy(grp, up, zs.at[0, 0]).start()
 
     @pl.when(jnp.logical_not(low))
     def _():
@@ -187,28 +205,9 @@
     got[me] = send[me]
     idgot[me] = idsend[me]
 
-    def token_down():
-        pl.semaphore_wait(token.at[1], 1)
-
-        @pl.when(jnp.logical_not(low))
-        def _():
-            pl.semaphore_signal(token.at[1], 1, device_id=(down, me), device_id_type=MESH)
-
-    @pl.when(jnp.logical_not(low))
-    def _():
-        pl.semaphore_wait(token.at[0], 1)
-
-        @pl.when(jnp.logical_not(high))
-        def _():
-            pl.semaphore_signal(token.at[0], 1, device_id=(up, me), device_id_type=MESH)
-
-    @pl.when((z >= NZ // 2) & (z < NZ - 1))
+    @pl.when((z >= NZ // 4) & (z < NZ // 2))
     def _():
         token_down()
-
-    @pl.when(high)
-    def _():
-        tile_copy(grp, up, zs.at[0, 0]).start()
 
     reach = (NZ // 2, NZ // 2 - 1)
 
@@ -223,11 +222,11 @@
 
         tile_copy(entry, twin, ks.at[way, step]).start()
 
-    @pl.loop(1, NZ // 2 + 4)
+    @pl.loop(1, NZ // 2 + 2)
     def _(t):
         for late in range(2):
             for way in range(2):
-                step = t - 3 * late
+                step = t - late
                 if (late, way) == (0, 1):
                     step -= low.astype(I32)
                 inside = (z, NZ - 1 - z)[way]
@@ -237,7 +236,7 @@
                 def _():
                     forward(way, step)
 
-        @pl.when((t == 1) & (z < NZ // 2))
+        @pl.when((t == 1) & (z < NZ // 4))
         def _():
             token_down()
 

time: 140 us -> 139 us (level)
  the two profiles are of different devices: /device:TPU:209 before, /device:TPU:1 now
where the time goes in v5:
time: 139 us
  Pallas kernels  139 us (100%)
    pallas_call x1, Pallas kernels, on_device(): pl.pallas_call(kernel, out_shape=(jax.ShapeDtypeStruct((PTS, K * TILE), F...  137 us

profile of v5, /device:TPU:1, one launch (start us, length us, event | category | flops | bytes accessed | tf_op | source)
XLA Modules:
  0.0 139.2 jit_solution(4958715505358399749)
XLA Ops:
  0.6 136.7 %fused.1 = (f32[256,256]{1,0:T(8,128)}, f32[4,128,128]{2,1,0:T(8,128)}, f32[1,256]{1,0:T(1,128)}) custom-call(bf16[256,4096]{1,0:T(8,128)(2,1)} %pts_hbm.1, bf16[7,4,4096]{2,1,0:T(4,128)(2,1)} %bitcast.5, s32[2,32]{1,0:T(2,128)} %bitcast.6, s32[1,256]{1,0:T(1,128)} %bitcast.7, s32[1,256]{1,0:T(1,128)} %bitcast.8), custom_call_target="tpu_custom_call" | custom-call | tf_op jit(solution)/shard_map/fused/pallas_call | solution.py:443
  137.4 1.8 %deliver.1 = (f32[256,256]{1,0:T(8,128)}, f32[4,128,128]{2,1,0:T(8,128)}, f32[1,256]{1,0:T(1,128)}) custom-call(f32[256,256]{1,0:T(8,128)} %get-tuple-element.9.a, f32[4,128,128]{2,1,0:T(8,128)} %get-tuple-element.10.b, f32[1,256]{1,0:T(1,128)} %get-tuple-element.11.c), custom_call_target="tpu_custom_call" | custom-call | tf_op jit(solution)/shard_map/deliver/pallas_call | solution.py:476

commit v6 on v5

--- a/solution.py
+++ b/solution.py
@@ -55,7 +55,7 @@
     pts_hbm, cen, cand, asg, slt,
     out_scores, out_gram, out_best,
     send, got, tiles, csend, cgot, idsend, idgot, repsend, repgot,
-    ps, pr, ids_s, ids_r, zs, zr, ks, cs, cr, rs, rr, token, pts, fs,
+    ps, pr, ids_s, ids_r, zs, zr, ks, cs, cr, rs, rr, token, here, pts, fs,
 ):
     fetch = pltpu.make_async_copy(pts_hbm, pts, fs.at[0])
     fetch.start()
@@ -73,21 +73,27 @@
     twin = z * NC + (1 - core)
     low, high = z == 0, z == NZ - 1
 
+    last = (grp == 0) & (me == 0)
+    beside = (grp == 0) & (me != 0)
+    over = (grp == 1) & (me == 0)
+    above = (grp == NC) & (me == 0)
     barrier = pltpu.get_barrier_semaphore()
 
-    @pl.loop(1, NS)
-    def _(k):
-        pl.semaphore_signal(barrier, 1, device_id=(grp, peer(k)), device_id_type=MESH)
-
-    pl.semaphore_signal(barrier, 1, device_id=(twin, me), device_id_type=MESH)
-
-    @pl.when(jnp.logical_not(high))
-    def _():
-        pl.semaphore_signal(barrier, 1, device_id=(up, me), device_id_type=MESH)
-
-    @pl.when(jnp.logical_not(low))
-    def _():
-        pl.semaphore_signal(barrier, 1, device_id=(down, me), device_id_type=MESH)
+    @pl.when(jnp.logical_not(last))
+    def _():
+        @pl.loop(1, NS)
+        def _(k):
+            pl.semaphore_signal(barrier, 1, device_id=(grp, peer(k)), device_id_type=MESH)
+
+        pl.semaphore_signal(barrier, 1, device_id=(twin, me), device_id_type=MESH)
+
+        @pl.when(jnp.logical_not(high))
+        def _():
+            pl.semaphore_signal(barrier, 1, device_id=(up, me), device_id_type=MESH)
+
+        @pl.when(jnp.logical_not(low))
+        def _():
+            pl.semaphore_signal(barrier, 1, device_id=(down, me), device_id_type=MESH)
 
     def tile_copy(entry, dest, ssem):
         return pltpu.make_async_remote_copy(
@@ -138,8 +144,16 @@
 
     fetch.wait()
     build(0)
-    ends = low.astype(I32) + high.astype(I32)
-    pl.semaphore_wait(barrier, NS - 1 + 3 - ends)
+    fewer = (low | high).astype(I32) + (beside | over | above).astype(I32)
+    pl.semaphore_wait(barrier, NS - 1 + 3 - fewer)
+
+    @pl.when(last)
+    def _():
+        @pl.loop(1, NS)
+        def _(k):
+            pl.semaphore_signal(here, 1, device_id=(grp, peer(k)), device_id_type=MESH)
+
+        pl.semaphore_signal(here, 1, device_id=(twin, me), device_id_type=MESH)
 
     @pl.when(low)
     def _():
@@ -152,7 +166,9 @@
     def send_points(j):
         @pl.loop(jnp.where(j == 0, 1, 0), NY)
         def _(i):
-            point_copy(j * NY + i).start()
+            @pl.when(jnp.logical_not(beside & (peer(j * NY + i) == 0)))
+            def _():
+                point_copy(j * NY + i).start()
 
     send_points(0)
 
@@ -174,6 +190,10 @@
     @pl.when((z >= NZ // 2) & (z < NZ - 1))
     def _():
         token_down()
+
+    @pl.when(over)
+    def _():
+        pl.semaphore_wait(here, 1)
 
     mine = [cen[t].astype(F32) for t in range(TPG)] + [jnp.zeros((4, D), F32)]
     tiles[grp] = jnp.concatenate(mine, axis=0).astype(BF16)
@@ -190,6 +210,16 @@
     def _(j):
         build(j)
         send_points(j)
+
+    @pl.when(beside)
+    def _():
+        pl.semaphore_wait(here, 1)
+
+        @pl.loop(1, NS)
+        def _(k):
+            @pl.when(peer(k) == 0)
+            def _():
+                point_copy(k).start()
 
     ids = lax.dot_general(
         own * (member_row + 1).astype(F32), at_rank, NT, precision=HI, preferred_element_type=F32
@@ -251,8 +281,8 @@
     line = iota((NS * 8, NS), 0)
     wanted = jnp.zeros((NS * 8, 1), I32)
     for k in range(K):
-        here = line // 4 == iota((NS * 8, NS), 1) * K + k
-        wanted += jnp.sum(jnp.where(here, cand[k : k + 1], 0), axis=1, keepdims=True)
+        match = line // 4 == iota((NS * 8, NS), 1) * K + k
+        wanted += jnp.sum(jnp.where(match, cand[k : k + 1], 0), axis=1, keepdims=True)
     first = (wanted * 9363) >> 16
     code = first * 32 + (wanted - first * TPG) * 4 + lax.rem(iota((NS * 8, 1), 0), 4)
     pick = flag(code == iota((NS * 8, NG * 32), 1), BF16)
@@ -462,7 +492,7 @@
             dma((NS,)), dma((NS,)), dma((NS,)), dma((NS,)),
             dma((2, NZ // 2)), dma((NG,)), dma((2, NZ // 2 + 1)),
             dma((NS,)), dma((NS,)), dma((NS,)), dma((NS,)),
-            pltpu.SemaphoreType.REGULAR((2,)),
+            pltpu.SemaphoreType.REGULAR((2,)), pltpu.SemaphoreType.REGULAR,
             pltpu.VMEM((PTS, D), BF16), dma((1,)),
         ],
         compiler_params=pltpu.CompilerParams(

time: 139 us -> 139 us (level)
  no operation moved by 1% of the time
where the time goes in v6:
time: 139 us
  Pallas kernels  138 us (99%)
    pallas_call x1, Pallas kernels, on_device(): pl.pallas_call(kernel, out_shape=(jax.ShapeDtypeStruct((PTS, K * TILE), F...  136 us

profile of v6, /device:TPU:1, one launch (start us, length us, event | category | flops | bytes accessed | tf_op | source)
XLA Modules:
  0.0 138.8 jit_solution(12464449176960241382)
XLA Ops:
  0.6 136.3 %fused.1 = (f32[256,256]{1,0:T(8,128)}, f32[4,128,128]{2,1,0:T(8,128)}, f32[1,256]{1,0:T(1,128)}) custom-call(bf16[256,4096]{1,0:T(8,128)(2,1)} %pts_hbm.1, bf16[7,4,4096]{2,1,0:T(4,128)(2,1)} %bitcast.5, s32[2,32]{1,0:T(2,128)} %bitcast.6, s32[1,256]{1,0:T(1,128)} %bitcast.7, s32[1,256]{1,0:T(1,128)} %bitcast.8), custom_call_target="tpu_custom_call" | custom-call | tf_op jit(solution)/shard_map/fused/pallas_call | solution.py:473
  136.9 1.8 %deliver.1 = (f32[256,256]{1,0:T(8,128)}, f32[4,128,128]{2,1,0:T(8,128)}, f32[1,256]{1,0:T(1,128)}) custom-call(f32[256,256]{1,0:T(8,128)} %get-tuple-element.9.a, f32[4,128,128]{2,1,0:T(8,128)} %get-tuple-element.10.b, f32[1,256]{1,0:T(1,128)} %get-tuple-element.11.c), custom_call_target="tpu_custom_call" | custom-call | tf_op jit(solution)/shard_map/deliver/pallas_call | solution.py:506

commit v7 on v6

--- a/solution.py
+++ b/solution.py
@@ -306,7 +306,7 @@
 
     @pl.loop(1, NS)
     def _(k):
-        cen_copy(k).start()
+        cen_copy(NS - k).start()
 
     cgot[me] = csend[me]
 
@@ -443,7 +443,7 @@
 
     @pl.loop(0, NX - 1)
     def _(j):
-        column_scores(j)
+        column_scores(NX - 1 - j)
 
     @pl.loop(1, NS)
     def _(k):
@@ -457,7 +457,7 @@
     def _(k):
         rep_copy(k).wait_send()
 
-    column_scores(NX - 1)
+    column_scores(0)
 
 
 def deliver(a, b, c, out_a, out_b, out_c):

time: 139 us -> 142 us (1.022)
  Pallas kernels: 138 us -> 141 us
    pallas_call x1, Pallas kernels: 136 us -> 139 us  [on_device(): pl.pallas_call(kernel, out_shape=(jax.ShapeDtypeStruct((PTS, K * TILE), F...]
where the time goes in v7:
time: 142 us
  Pallas kernels  141 us (99%)
    pallas_call x1, Pallas kernels, on_device(): pl.pallas_call(kernel, out_shape=(jax.ShapeDtypeStruct((PTS, K * TILE), F...  139 us

profile of v7, /device:TPU:1, one launch (start us, length us, event | category | flops | bytes accessed | tf_op | source)
XLA Modules:
  0.0 141.7 jit_solution(14481407282888507837)
XLA Ops:
  0.6 139.2 %fused.1 = (f32[256,256]{1,0:T(8,128)}, f32[4,128,128]{2,1,0:T(8,128)}, f32[1,256]{1,0:T(1,128)}) custom-call(bf16[256,4096]{1,0:T(8,128)(2,1)} %pts_hbm.1, bf16[7,4,4096]{2,1,0:T(4,128)(2,1)} %bitcast.5, s32[2,32]{1,0:T(2,128)} %bitcast.6, s32[1,256]{1,0:T(1,128)} %bitcast.7, s32[1,256]{1,0:T(1,128)} %bitcast.8), custom_call_target="tpu_custom_call" | custom-call | tf_op jit(solution)/shard_map/fused/pallas_call | solution.py:473
  139.8 1.8 %deliver.1 = (f32[256,256]{1,0:T(8,128)}, f32[4,128,128]{2,1,0:T(8,128)}, f32[1,256]{1,0:T(1,128)}) custom-call(f32[256,256]{1,0:T(8,128)} %get-tuple-element.9.a, f32[4,128,128]{2,1,0:T(8,128)} %get-tuple-element.10.b, f32[1,256]{1,0:T(1,128)} %get-tuple-element.11.c), custom_call_target="tpu_custom_call" | custom-call | tf_op jit(solution)/shard_map/deliver/pallas_call | solution.py:506
